TPU v7x, 32 devices: a whole 2x2x4 slice. The times are simulated.
32 devices in a mesh: row: 8 (over z, core), col: 4 (over y, x).
Axes of the slice: x: 2, y: 2, z: 4, core: 2. Of those that a mesh axis runs over, the one named last changes fastest.
Arguments:
- covariance: float32 [8192, 8192], P('row', 'col'), may hold values from -3 to 5, as said below
- obs_cells: int32 [2, 8192], P(None, ('row', 'col')), may hold values from 0 to 255
- pred_cells: int32 [2, 512], replicated, may hold values from 0 to 255
- targets: float32 [8192, 256], P(('row', 'col')), may hold values from -1.5 to 1.5
- cross_sum: float32 [8192, 512], P(('row', 'col')), may hold values from -1.8 to 1.8
- prior_mean: float32 [512, 256], replicated, may hold values from -6 to 6
Outputs:
- factor_state: float32 [8192, 8192], P('row', 'col')
- reduced_targets: float32 [8192, 256], P(('row', 'col'))
- cross_next: float32 [8192, 512], P(('row', 'col'))
- predicted: float32 [512, 256], replicated
Inputs may be any that keep to these rules, and one draw needn't show every extreme that they name: covariance is symmetric and positive definite.
All inputs are finite; a program needn't handle non-finite values.
Results may differ from a plain program's by a relative error of at most 0.00007.
Values sent between devices are 32-bit elements; how exact they have to be, the bound alone decides.
A program may use at most 128 MiB of HBM per device.

v0:
```python
import math

import jax
import jax.numpy as jnp
from jax import lax
from jax.sharding import PartitionSpec as P

RANGE = 16


root_three = math.sqrt(3.0)


def spread(block, axis, source):
    block = jnp.where(lax.axis_index(axis) == source, block, jnp.zeros_like(block))
    return lax.psum(block, axis)


def matern_tile(first, second):
    delta_x = first[0][:, None] - second[0][None, :]
    delta_y = first[1][:, None] - second[1][None, :]
    scaled = jnp.sqrt(delta_x * delta_x + delta_y * delta_y) * (root_three / RANGE)
    return (1.0 + scaled) * jnp.exp(-scaled)


def right_solve(factor, block):
    return lax.linalg.triangular_solve(factor, block, left_side=False, lower=True, transpose_a=True)


def body(covariance, obs_cells, pred_cells, targets, cross_sum, prior_mean):
    tile_size = covariance.shape[0]
    per_col = covariance.shape[1] // tile_size
    slab = targets.shape[0]
    row_index = lax.axis_index("row")
    column_index = lax.axis_index("col")
    cells_float = obs_cells.astype(jnp.float32)
    panel_in = spread(covariance[:, :tile_size], "col", 0)
    diag_in, top_cov, top_targets, top_cross, top_cells = (
        spread(panel_in, "row", 0),
        spread(covariance, "row", 0),
        spread(targets, "row", 0),
        spread(cross_sum, "row", 0),
        spread(cells_float, "row", 0),
    )
    lead_factor = jnp.linalg.cholesky(diag_in)
    panel_rows = right_solve(lead_factor, panel_in)
    column_tiles = []
    for offset in range(per_col):
        raw_tile = top_cov[:, offset * tile_size : (offset + 1) * tile_size]
        column_tiles.append(right_solve(lead_factor, raw_tile.T))
    blocks = []
    for offset in range(per_col):
        local = covariance[:, offset * tile_size : (offset + 1) * tile_size]
        updated = local - jnp.dot(
            panel_rows, column_tiles[offset].T, precision=lax.Precision.HIGHEST
        )
        global_col = per_col * column_index + offset
        updated = jnp.where(row_index == 0, jnp.zeros_like(updated), updated)
        updated = jnp.where(global_col == 0, panel_rows, updated)
        blocks.append(updated)
    factor_state = jnp.concatenate(blocks, axis=1)
    lead_targets, lead_cross, lead_cells = (
        lax.all_gather(top_targets, "col", axis=0, tiled=True),
        lax.all_gather(top_cross, "col", axis=0, tiled=True),
        lax.all_gather(top_cells, "col", axis=1, tiled=True),
    )
    kernel = matern_tile(lead_cells, pred_cells.astype(jnp.float32))
    stacked = jnp.concatenate([lead_targets, kernel - lead_cross], axis=1)
    both = lax.linalg.triangular_solve(
        lead_factor, stacked, left_side=True, lower=True, transpose_a=False
    )
    width = targets.shape[1]
    solved = both[:, :width]
    lifted = both[:, width:]
    my_rows = lax.dynamic_slice_in_dim(panel_rows, column_index * slab, slab, 0)
    my_solved = lax.dynamic_slice_in_dim(solved, column_index * slab, slab, 0)
    my_lifted = lax.dynamic_slice_in_dim(lifted, column_index * slab, slab, 0)
    reduced_targets = targets - jnp.dot(my_rows, solved, precision=lax.Precision.HIGHEST)
    reduced_targets = jnp.where(row_index == 0, my_solved, reduced_targets)
    cross_next = cross_sum + jnp.dot(my_rows, lifted, precision=lax.Precision.HIGHEST)
    cross_next = jnp.where(row_index == 0, my_lifted, cross_next)
    predicted = prior_mean + lax.dot_general(
        lifted, solved, (((0,), (0,)), ((), ())), precision=lax.Precision.HIGHEST
    )
    return (factor_state, reduced_targets, cross_next, predicted)


def solution(mesh):
    in_specs = (
        P("row", "col"),
        P(None, ("row", "col")),
        P(),
        P(("row", "col"), None),
        P(("row", "col"), None),
        P(),
    )
    out_specs = (P("row", "col"), P(("row", "col"), None), P(("row", "col"), None), P())
    return jax.shard_map(body, mesh=mesh, in_specs=in_specs, out_specs=out_specs, check_vma=False)
```

profile of v0, /device:TPU:29, one launch (start us, length us, event | category | flops | bytes accessed | tf_op | source)
XLA Modules:
  0.0 890.0 jit_solution(1839362975442033429)
XLA Ops:
  7.2 8.5 fusion.205
  15.7 5.4 copy.40
  21.1 2.8 broadcast_select_fusion.2
  26.4 5.0 broadcast_select_fusion
  31.4 97.6 %all-reduce.5.cloned.1.call-done = f32[1024,1024]{0,1:T(8,128)} async-done(((f32[1024,1024]{0,1:T(8,128)}), f32[1024,1024]{0,1:T(8,128)}) %all-reduce.5.cloned.1.call-update) | async-done | bytes 4194320 | tf_op jit(solution)/shard_map/psum | solution.py:16
  129.0 2.8 broadcast_select_fusion.1
  131.9 5.3 copy.41
  137.2 13.4 %psum.46 = f32[2,256]{1,0:T(2,128)S(1)} all-reduce(f32[2,256]{1,0:T(2,128)S(1)} %convert_select_fusion), channel_id=1, replica_groups=mesh['row'=8,'col'=4] {'row'}, use_global_device_ids=true, to_apply=%region_20.22 | all-reduce | flops 512 | bytes 4096 | tf_op jit(solution)/shard_map/psum | solution.py:16
  150.6 5.9 all_gather.10
  156.6 246.3 %all-reduce.7.cloned.1.call-done = (f32[1024,1024]{0,1:T(8,128)}, f32[1024,2048]{1,0:T(8,128)}, f32[256,512]{1,0:T(8,128)}, f32[256,256]{1,0:T(8,128)}) async-done(((f32[1024,1024]{0,1:T(8,128)}, f32[1024,2048]{1,0:T(8,128)}, f32[256,512]{1,0:T(8,128)}, f32[256,256]{1,0:T(8,128)}), (f32[1024,1024]{0,1:T(8,128)}, f32[1024,2048]{1,0:T(8,128)}, f32[256,512]{1,0:T(8,128)}, ...) | async-done | bytes 13369360 | tf_op jit(solution)/shard_map/psum | solution.py:16
  402.8 5.5 copy.11
  408.4 4.4 fusion
  414.8 11.7 %cholesky.222 = f32[128,128]{1,0:T(8,128)S(1)} custom-call(f32[128,128]{1,0:T(8,128)S(1)} %cholesky.577), custom_call_target="Cholesky" | custom-call | tf_op jit(solution)/shard_map/jit(cholesky)/cholesky | solution.py:45
  426.7 9.8 %custom-call.65 = f32[1,128,128]{1,2,0:T(8,128)S(1)} custom-call(f32[1,128,128]{2,1,0:T(8,128)S(1)} %get-tuple-element.187), custom_call_target="InvertDiagBlocksLowerTriangular" | custom-call | tf_op jit(solution)/shard_map/jit(cholesky)/cholesky | solution.py:45
  439.8 11.7 %cholesky.243 = f32[128,128]{1,0:T(8,128)S(1)} custom-call(f32[128,128]{1,0:T(8,128)S(1)} %cholesky.581), custom_call_target="Cholesky" | custom-call | tf_op jit(solution)/shard_map/jit(cholesky)/cholesky | solution.py:45
  452.1 9.8 %custom-call.66 = f32[1,128,128]{1,2,0:T(8,128)S(1)} custom-call(f32[1,128,128]{2,1,0:T(8,128)S(1)} %get-tuple-element.185), custom_call_target="InvertDiagBlocksLowerTriangular" | custom-call | tf_op jit(solution)/shard_map/jit(cholesky)/cholesky | solution.py:45
  467.4 11.7 %cholesky.466 = f32[128,128]{1,0:T(8,128)S(1)} custom-call(f32[128,128]{1,0:T(8,128)S(1)} %cholesky.586), custom_call_target="Cholesky" | custom-call | tf_op jit(solution)/shard_map/jit(cholesky)/cholesky | solution.py:45
  479.9 9.8 %custom-call.67 = f32[1,128,128]{1,2,0:T(8,128)S(1)} custom-call(f32[1,128,128]{2,1,0:T(8,128)S(1)} %get-tuple-element.183), custom_call_target="InvertDiagBlocksLowerTriangular" | custom-call | tf_op jit(solution)/shard_map/jit(cholesky)/cholesky | solution.py:45
  490.9 3.3 convolution_subtract_fusion.23
  494.3 11.7 %cholesky.485 = f32[128,128]{1,0:T(8,128)S(1)} custom-call(f32[128,128]{1,0:T(8,128)S(1)} %cholesky.591), custom_call_target="Cholesky" | custom-call | tf_op jit(solution)/shard_map/jit(cholesky)/cholesky | solution.py:45
  506.8 9.8 %custom-call.68 = f32[1,128,128]{1,2,0:T(8,128)S(1)} custom-call(f32[1,128,128]{2,1,0:T(8,128)S(1)} %get-tuple-element.181), custom_call_target="InvertDiagBlocksLowerTriangular" | custom-call | tf_op jit(solution)/shard_map/jit(cholesky)/cholesky | solution.py:45
  517.7 3.2 convolution_subtract_fusion.25
  520.9 12.1 %cholesky.504 = f32[128,128]{1,0:T(8,128)S(1)} custom-call(f32[128,128]{1,0:T(8,128)S(1)} %cholesky.596), custom_call_target="Cholesky" | custom-call | tf_op jit(solution)/shard_map/jit(cholesky)/cholesky | solution.py:45
  533.8 9.8 %custom-call.69 = f32[1,128,128]{1,2,0:T(8,128)S(1)} custom-call(f32[1,128,128]{2,1,0:T(8,128)S(1)} %get-tuple-element.179), custom_call_target="InvertDiagBlocksLowerTriangular" | custom-call | tf_op jit(solution)/shard_map/jit(cholesky)/cholesky | solution.py:45
  544.7 3.2 convolution_subtract_fusion.26
  547.9 11.7 %cholesky.524 = f32[128,128]{1,0:T(8,128)S(1)} custom-call(f32[128,128]{1,0:T(8,128)S(1)} %cholesky.601), custom_call_target="Cholesky" | custom-call | tf_op jit(solution)/shard_map/jit(cholesky)/cholesky | solution.py:45
  560.4 9.8 %custom-call.70 = f32[1,128,128]{1,2,0:T(8,128)S(1)} custom-call(f32[1,128,128]{2,1,0:T(8,128)S(1)} %get-tuple-element.177), custom_call_target="InvertDiagBlocksLowerTriangular" | custom-call | tf_op jit(solution)/shard_map/jit(cholesky)/cholesky | solution.py:45
  571.2 2.8 convolution_subtract_fusion.27
  574.0 11.7 %cholesky.544 = f32[128,128]{1,0:T(8,128)S(1)} custom-call(f32[128,128]{1,0:T(8,128)S(1)} %cholesky.606), custom_call_target="Cholesky" | custom-call | tf_op jit(solution)/shard_map/jit(cholesky)/cholesky | solution.py:45
  586.5 9.8 %custom-call.71 = f32[1,128,128]{1,2,0:T(8,128)S(1)} custom-call(f32[1,128,128]{2,1,0:T(8,128)S(1)} %get-tuple-element.175), custom_call_target="InvertDiagBlocksLowerTriangular" | custom-call | tf_op jit(solution)/shard_map/jit(cholesky)/cholesky | solution.py:45
  599.3 11.7 %cholesky.562 = f32[128,128]{1,0:T(8,128)S(1)} custom-call(f32[128,128]{1,0:T(8,128)S(1)} %convolution_subtract_fusion.28), custom_call_target="Cholesky" | custom-call | tf_op jit(solution)/shard_map/jit(cholesky)/cholesky | solution.py:45
  621.4 4.9 select_select_fusion
  626.3 24.1 %while.7 = (s32[]{:T(128)}, f32[1024,1024]{0,1:T(8,128)}, s32[8,2]{0,1:T(2,128)S(1)}, f32[8,128,128]{2,1,0:T(8,128)S(1)}, s32[]{:T(128)}) while((s32[]{:T(128)}, f32[1024,1024]{0,1:T(8,128)}, s32[8,2]{0,1:T(2,128)S(1)}, f32[8,128,128]{2,1,0:T(8,128)S(1)}, s32[]{:T(128)}) %tuple.139), condition=%wide.while_cond, body=%wide.while_body.sunk | while | flops 2 | bytes 393329 | solution.py:27
  650.4 79.0 %custom-call.75 = f32[8,128,128]{1,2,0:T(8,128)S(1)} custom-call(f32[8,128,128]{2,1,0:T(8,128)S(1)} %get-tuple-element.33), custom_call_target="InvertDiagBlocksLowerTriangular" | custom-call | tf_op jit(solution)/shard_map/triangular_solve/custom-call.7 | solution.py:27
  729.4 4.3 slice_bitcast_fusion.1
  744.9 2.8 convolution_subtract_fusion.6
  748.4 3.2 convolution_subtract_fusion.3
  752.2 3.8 convolution_subtract_fusion.9
  801.7 19.9 %select_select_fusion.2 = f32[1024,1024]{0,1:T(8,128)S(1)} fusion(f32[1024,1024]{0,1:T(8,128)} %copy-done.3, f32[1024,1024]{0,1:T(8,128)} %copy.40, pred[]{:T(512)S(6)} %eq.9, pred[]{:T(512)S(6)} %eq.8, f32[1024,1024]{0,1:T(8,128)} %convolution_dynamic-update-slice_fusion.1), kind=kOutput, calls=%fused_computation.24 | convolution fusion | flops 12888047616 | bytes 16777218 | tf_op jit(solution)/shard_map/dot_general | solution.py:54
  821.6 13.8 %select_select_fusion.1 = f32[1024,1024]{0,1:T(8,128)S(1)} fusion(f32[1024,1024]{0,1:T(8,128)S(1)} %copy-done.4, f32[1024,1024]{0,1:T(8,128)S(1)} %copy-done.6, pred[]{:T(512)S(6)} %eq.11, pred[]{:T(512)S(6)} %eq.9, f32[1024,1024]{0,1:T(8,128)S(1)} %copy-done.12), kind=kOutput, calls=%fused_computation.23 | convolution fusion | flops 12888047616 | bytes 16777218 | tf_op jit(solution)/shard_map/dot_general | solution.py:54
  835.5 4.1 pad_maximum_fusion
  839.6 9.1 %copy.32 = f32[1024,2048]{1,0:T(8,128)} copy(f32[1024,2048]{0,1:T(8,128)} %pad_maximum_fusion) | data formatting | bytes 16777216
  848.7 2.9 multiply_subtract_fusion
  865.2 2.5 convolution_subtract_fusion.20
  868.2 3.1 convolution_subtract_fusion.16
  873.5 2.6 fusion.78
  876.1 2.9 fusion.51
  879.0 4.3 convolution_add_fusion
  (210 shorter events, 128.6 us)
Async XLA Ops:
  7.2 121.8 %all-reduce.5.cloned.1.call-start = ((), (), s32[]{:S(2)}) async-start(), calls=%async_computation | async-start | bytes 8388608 | tf_op jit(solution)/shard_map/psum | solution.py:16
  23.9 0.9 copy-start.18
  23.9 1.7 copy-start.16
  23.9 378.9 %all-reduce.7.cloned.1.call-start = ((), (), s32[]{:S(2)}) async-start(), calls=%async_computation.3 | async-start | bytes 26738688 | tf_op jit(solution)/shard_map/psum | solution.py:16
  131.8 716.9 %all-gather.5.cloned.1.call-start = ((), (), s32[]{:S(2)}) async-start(), calls=%async_computation.2 | async-start | bytes 2621440 | tf_op jit(solution)/shard_map/all_gather | solution.py:64
  131.8 5.4 copy-start.20
  131.8 5.4 copy-start.21
  412.8 2.0 copy-start.10
  463.0 2.0 copy-start.1
  733.7 24.3 %copy-start.8 = (f32[1024,1024]{0,1:T(8,128)}, f32[1024,1024]{0,1:T(8,128)S(1)}, u32[]{:S(2)}) copy-start(f32[1024,1024]{0,1:T(8,128)S(1)} %get-tuple-element.70) | copy-start | bytes 12582916
  752.1 5.9 copy-start.11
  759.5 92.2 %all-gather.3.cloned.1.call-start = ((), (), s32[]{:S(2)}) async-start(), calls=%async_computation.1 | async-start | bytes 1310720 | tf_op jit(solution)/shard_map/all_gather | solution.py:63
  759.6 4.4 copy-start.2
  763.2 3.6 copy-start.7
  773.3 6.2 copy-start.15
  775.4 4.2 copy-start.13
  775.4 4.2 copy-start.14
  776.4 5.1 copy-start.9
  779.5 4.3 copy-start.3
  801.7 19.9 %copy-start.4 = (f32[1024,1024]{0,1:T(8,128)S(1)}, f32[1024,1024]{0,1:T(8,128)}, u32[]{:S(2)}) copy-start(f32[1024,1024]{0,1:T(8,128)} %copy-done.3) | copy-start | bytes 12582916
  801.7 19.9 %copy-start.6 = (f32[1024,1024]{0,1:T(8,128)S(1)}, f32[1024,1024]{0,1:T(8,128)}, u32[]{:S(2)}) copy-start(f32[1024,1024]{0,1:T(8,128)} %copy.41) | copy-start | bytes 12582916
  801.7 19.9 %copy-start.12 = (f32[1024,1024]{0,1:T(8,128)S(1)}, f32[1024,1024]{0,1:T(8,128)}, u32[]{:S(2)}) copy-start(f32[1024,1024]{0,1:T(8,128)} %convolution_dynamic-update-slice_fusion) | copy-start | bytes 12582916
  851.7 1.6 copy-start
  871.3 2.2 copy-start.5
  871.9 4.2 copy-start.17
  873.5 5.5 copy-start.19
Sparse Core Ops, SparseCore 0:
  24.0 104.9 all-reduce.4
  132.4 270.4 all-reduce.6
  759.6 36.0 all-gather.4
  801.8 27.3 all-gather.2
where the time goes:
time: 898 us; the launch traced here: 890 us
  waiting for transfers between devices  344 us (38%)
  other arithmetic  275 us (31%)
  matrix products  157 us (17%)
  local copies, waits for them, and re-layouts  74 us (8%)
  between operations  20 us (2%)
  blocking collectives  19.3 us (2%)
    psum x2, waiting for transfers between devices, spread(): return lax.psum(block, axis)  344 us
    another operation x30, other arithmetic, body(): lead_factor = jnp.linalg.cholesky(diag_in)  168 us
    another operation x4, other arithmetic, right_solve(): lax.linalg.triangular_solve(factor, block, left_side=False, lower=True, t...  83.9 us
    another operation x45, matrix products, right_solve(): lax.linalg.triangular_solve(factor, block, left_side=False, lower=True, t...  67.4 us
    dot_general x2, matrix products, body(): jnp.dot(panel_rows, column_tiles[offset].T, precision=lax.Precision.HIGHEST)  33.7 us
    unnamed x47, local copies, waits for them, and re-layouts  26 us
    another operation x14, matrix products, body(): lead_factor = jnp.linalg.cholesky(diag_in)  25.9 us
    another operation x41, local copies, waits for them, and re-layouts, right_solve(): lax.linalg.triangular_solve(factor, block, left_side=False, lower=True, t...  23.8 us
  transfers between devices with their start and end apart: 4, of which 2 were waited for; matrix products, arithmetic and copies ran while one was open for 12% of the time, Pallas kernels for 0%

commit v1 on v0

v1 whole, which is shorter than its diff:
```python
import math

import jax
import jax.numpy as jnp
from jax import lax
from jax.experimental import pallas as pl
from jax.experimental.pallas import tpu as pltpu
from jax.sharding import PartitionSpec as P

RANGE = 16
BLOCK = 128
GROUP = 8


root_three = math.sqrt(3.0)


def invert_block(block):
    size = block.shape[0]
    groups = size // GROUP
    rows = lax.broadcasted_iota(jnp.int32, (GROUP, size), 0)
    columns = lax.broadcasted_iota(jnp.int32, (GROUP, size), 1)
    left = [block[g * GROUP : (g + 1) * GROUP, :] for g in range(groups)]
    right = [jnp.where(columns == rows + g * GROUP, 1.0, 0.0) for g in range(groups)]
    for g in range(groups):
        first = g * GROUP
        more = g + 1 < groups
        wide = (GROUP, size)
        own = [jnp.broadcast_to(left[g][:, first + k : first + k + 1], wide) for k in range(GROUP)]
        if more:
            following = [
                jnp.broadcast_to(left[g + 1][:, first + k : first + k + 1], wide) for k in range(GROUP)
            ]
        for k in range(GROUP):
            root = lax.rsqrt(jnp.broadcast_to(own[k][k : k + 1, :], wide))
            factor = own[k] * root
            row_left = jnp.broadcast_to(left[g][k : k + 1, :], wide) * root
            row_right = jnp.broadcast_to(right[g][k : k + 1, :], wide) * root
            below = rows > k
            here = rows == k

            def step(old, row):
                return jnp.where(below, old - factor * row, jnp.where(here, row, old))

            if more:
                factor_next = following[k] * root
            for m in range(k + 1, GROUP):
                row = jnp.broadcast_to(own[m][k : k + 1, :], wide) * root
                own[m] = jnp.where(below, own[m] - factor * row, own[m])
                if more:
                    following[m] = following[m] - factor_next * row
            left[g] = step(left[g], row_left)
            right[g] = step(right[g], row_right)
            if more:
                left[g + 1] = left[g + 1] - factor_next * row_left
                right[g + 1] = right[g + 1] - factor_next * row_right
        if g + 2 < groups:
            turned = left[g].T
            for i in range(g + 2, groups):
                for k in range(GROUP):
                    factor = jnp.broadcast_to(turned[i * GROUP : (i + 1) * GROUP, k : k + 1], wide)
                    left[i] = left[i] - factor * jnp.broadcast_to(left[g][k : k + 1, :], wide)
                    right[i] = right[i] - factor * jnp.broadcast_to(right[g][k : k + 1, :], wide)
    return jnp.concatenate(right, axis=0)


def invert_kernel(lead_ref, inverse_ref, work):
    size = lead_ref.shape[0]
    count = size // BLOCK
    work[...] = lead_ref[...]
    columns = lax.broadcasted_iota(jnp.int32, (BLOCK, size), 1)

    @pl.loop(0, count)
    def _(j):
        at = pl.ds(pl.multiple_of(j * BLOCK, BLOCK), BLOCK)
        inverse = invert_block(work[at, at])
        pivot = jnp.dot(inverse, work[at, :], precision=lax.Precision.HIGHEST)
        work[at, :] = pivot
        work[at, at] = inverse
        inverse_ref[at, :] = jnp.where(columns < (j + 1) * BLOCK, work[at, :], 0.0)

        @pl.loop(j + 1, count)
        def _(i):
            to = pl.ds(pl.multiple_of(i * BLOCK, BLOCK), BLOCK)
            factor = work[at, to]
            work[to, at] = jnp.zeros((BLOCK, BLOCK), jnp.float32)
            work[to, :] = work[to, :] - lax.dot_general(
                factor, work[at, :], (((0,), (0,)), ((), ())), precision=lax.Precision.HIGHEST
            )


def invert_factor(lead):
    size = lead.shape[0]
    return pl.pallas_call(
        invert_kernel,
        out_shape=jax.ShapeDtypeStruct((size, size), jnp.float32),
        in_specs=[pl.BlockSpec(memory_space=pltpu.VMEM)],
        out_specs=pl.BlockSpec(memory_space=pltpu.VMEM),
        scratch_shapes=[pltpu.VMEM((size, size), jnp.float32)],
        compiler_params=pltpu.CompilerParams(vmem_limit_bytes=40 * 2**20),
    )(lead)


def spread(block, axis, source):
    block = jnp.where(lax.axis_index(axis) == source, block, jnp.zeros_like(block))
    return lax.psum(block, axis)


def matern_tile(first, second):
    delta_x = first[0][:, None] - second[0][None, :]
    delta_y = first[1][:, None] - second[1][None, :]
    scaled = jnp.sqrt(delta_x * delta_x + delta_y * delta_y) * (root_three / RANGE)
    return (1.0 + scaled) * jnp.exp(-scaled)


def dot(first, second, first_axis, second_axis):
    return lax.dot_general(
        first, second, (((first_axis,), (second_axis,)), ((), ())), precision=lax.Precision.HIGH
    )


def body(covariance, obs_cells, pred_cells, targets, cross_sum, prior_mean):
    tile_size = covariance.shape[0]
    slab = targets.shape[0]
    row_index = lax.axis_index("row")
    column_index = lax.axis_index("col")
    cells_float = obs_cells.astype(jnp.float32)
    panel_in = spread(covariance[:, :tile_size], "col", 0)
    diag_in, top_cov, top_targets, top_cross, top_cells = (
        spread(panel_in, "row", 0),
        spread(covariance, "row", 0),
        spread(targets, "row", 0),
        spread(cross_sum, "row", 0),
        spread(cells_float, "row", 0),
    )
    inverse = invert_factor(diag_in)
    panel_rows = dot(panel_in, inverse, 1, 1)
    panel_columns = dot(inverse, top_cov, 1, 0)
    updated = covariance - dot(panel_rows, panel_columns, 1, 0)
    updated = jnp.where(row_index == 0, jnp.zeros_like(updated), updated)
    first_tile = jnp.where(column_index == 0, panel_rows, updated[:, :tile_size])
    factor_state = jnp.concatenate([first_tile, updated[:, tile_size:]], axis=1)
    lead_targets, lead_cross, lead_cells = (
        lax.all_gather(top_targets, "col", axis=0, tiled=True),
        lax.all_gather(top_cross, "col", axis=0, tiled=True),
        lax.all_gather(top_cells, "col", axis=1, tiled=True),
    )
    kernel = matern_tile(lead_cells, pred_cells.astype(jnp.float32))
    stacked = jnp.concatenate([lead_targets, kernel - lead_cross], axis=1)
    both = dot(inverse, stacked, 1, 0)
    width = targets.shape[1]
    solved = both[:, :width]
    lifted = both[:, width:]
    my_rows = lax.dynamic_slice_in_dim(panel_rows, column_index * slab, slab, 0)
    my_solved = lax.dynamic_slice_in_dim(solved, column_index * slab, slab, 0)
    my_lifted = lax.dynamic_slice_in_dim(lifted, column_index * slab, slab, 0)
    reduced_targets = targets - dot(my_rows, solved, 1, 0)
    reduced_targets = jnp.where(row_index == 0, my_solved, reduced_targets)
    cross_next = cross_sum + dot(my_rows, lifted, 1, 0)
    cross_next = jnp.where(row_index == 0, my_lifted, cross_next)
    predicted = prior_mean + dot(lifted, solved, 0, 0)
    return (factor_state, reduced_targets, cross_next, predicted)


def solution(mesh):
    in_specs = (
        P("row", "col"),
        P(None, ("row", "col")),
        P(),
        P(("row", "col"), None),
        P(("row", "col"), None),
        P(),
    )
    out_specs = (P("row", "col"), P(("row", "col"), None), P(("row", "col"), None), P())
    return jax.shard_map(body, mesh=mesh, in_specs=in_specs, out_specs=out_specs, check_vma=False)
```

time: 898 us -> 564 us (0.63)
  other arithmetic: 275 us -> 26.2 us
  matrix products: 157 us -> 55.3 us
  local copies, waits for them, and re-layouts: 74 us -> 14.5 us
  Pallas kernels: 0 us -> 58.4 us
  waiting for transfers between devices: 344 us -> 368 us
    another operation x34 -> x0, other arithmetic: 252 us -> none  [the longest x30 168 us: body(): lead_factor = jnp.linalg.cholesky(diag_in)]
    another operation x74 -> x0, matrix products: 113 us -> none  [the longest x45 67.4 us: right_solve(): lax.linalg.triangular_solve(factor, block, left_side=False, lower=True, t...]
    pallas_call x0 -> x1, Pallas kernels: none -> 58.4 us  [invert_factor(): pl.pallas_call(invert_kernel, out_shape=jax.ShapeDtypeStruct((size, size)...]
    another operation x66 -> x0, local copies, waits for them, and re-layouts: 29.3 us -> none  [the longest x41 23.8 us: right_solve(): lax.linalg.triangular_solve(factor, block, left_side=False, lower=True, t...]
    psum x2, waiting for transfers between devices: 344 us -> 368 us  [spread(): return lax.psum(block, axis)]
    unnamed x47 -> x22, local copies, waits for them, and re-layouts: 26 us -> 8.77 us
    dot_general x5 -> x7, matrix products: 43.5 us -> 55.3 us  [dot(): lax.dot_general(first, second, (((first_axis,), (second_axis,)), ((), ())...]
  transfers between devices with their start and end apart: 4 -> 4, of which waited for: 2 -> 2; matrix products, arithmetic and copies ran while one was open for 12% -> 12% of each run, Pallas kernels for 0% -> 11%
where the time goes in v1:
time: 564 us; the launch traced here: 556 us
  waiting for transfers between devices  368 us (65%)
  Pallas kernels  58.4 us (10%)
  matrix products  55.3 us (10%)
  other arithmetic  26.2 us (5%)
  blocking collectives  19.4 us (3%)
  local copies, waits for them, and re-layouts  14.5 us (3%)
  between operations  14 us (2%)
    psum x2, waiting for transfers between devices, spread(): return lax.psum(block, axis)  368 us
    pallas_call x1, Pallas kernels, invert_factor(): pl.pallas_call(invert_kernel, out_shape=jax.ShapeDtypeStruct((size, size)...  58.4 us
    dot_general x7, matrix products, dot(): lax.dot_general(first, second, (((first_axis,), (second_axis,)), ((), ())...  55.3 us
    select_n x6, other arithmetic, spread(): jnp.where(lax.axis_index(axis) == source, block, jnp.zeros_like(block))  14.4 us
    psum x1, blocking collectives, spread(): return lax.psum(block, axis)  13.1 us
  transfers between devices with their start and end apart: 4, of which 2 were waited for; matrix products, arithmetic and copies ran while one was open for 12% of the time, Pallas kernels for 11%

profile of v1, /device:TPU:29, one launch (start us, length us, event | category | flops | bytes accessed | tf_op | source)
XLA Modules:
  0.0 555.9 jit_solution(12972473303279626823)
XLA Ops:
  7.2 0.0 all-reduce.4.cloned.1.call-start
  7.2 5.0 slice_select_fusion.1
  12.2 0.0 all-reduce.4.cloned.1.call-update
  12.2 0.0 all-reduce.6.cloned.1.call-start
  12.3 0.9 copy-done.7
  13.1 0.7 broadcast_select_fusion.3
  13.9 0.0 copy-done.6
  13.9 0.8 broadcast_select_fusion.2
  14.7 5.1 broadcast_select_fusion
  19.8 97.2 %all-reduce.4.cloned.1.call-done = f32[1024,1024]{1,0:T(8,128)} async-done(((f32[1024,1024]{1,0:T(8,128)}), f32[1024,1024]{1,0:T(8,128)}) %all-reduce.4.cloned.1.call-update) | async-done | bytes 4194320 | tf_op jit(solution)/shard_map/psum | solution.py:106
  117.0 2.8 broadcast_select_fusion.1
  119.8 0.0 all-reduce.6.cloned.1.call-update
  119.8 0.0 all-gather.5.cloned.1.call-start
  119.8 270.7 %all-reduce.6.cloned.1.call-done = (f32[1024,1024]{1,0:T(8,128)}, f32[1024,2048]{1,0:T(8,128)}, f32[256,512]{1,0:T(8,128)}, f32[256,256]{1,0:T(8,128)}) async-done(((f32[1024,1024]{1,0:T(8,128)}, f32[1024,2048]{1,0:T(8,128)}, f32[256,512]{1,0:T(8,128)}, f32[256,256]{1,0:T(8,128)}), (f32[1024,1024]{1,0:T(8,128)}, f32[1024,2048]{1,0:T(8,128)}, f32[256,512]{1,0:T(8,128)}, ...) | async-done | bytes 13369360 | tf_op jit(solution)/shard_map/psum | solution.py:106
  390.5 0.0 all-gather.5.cloned.1.call-update
  390.6 0.0 all-gather.3.cloned.1.call-start
  390.6 0.0 copy-done.9
  390.6 0.0 copy-done.10
  390.7 13.1 %psum.46 = f32[2,256]{1,0:T(2,128)S(1)} all-reduce(f32[2,256]{1,0:T(2,128)S(1)} %convert_select_fusion), channel_id=1, replica_groups=mesh['row'=8,'col'=4] {'row'}, use_global_device_ids=true, to_apply=%region_4.5 | all-reduce | flops 512 | bytes 4096 | tf_op jit(solution)/shard_map/psum | solution.py:106
  403.7 6.3 %all_gather.10 = f32[2,1024]{1,0:T(2,128)S(1)} all-gather(f32[2,256]{1,0:T(2,128)S(1)} %psum.46), channel_id=1, replica_groups=mesh['row'=8,'col'=4] {'col'}, dimensions={1}, use_global_device_ids=true | all-gather | bytes 10240 | tf_op jit(solution)/shard_map/all_gather | solution.py:146
  410.0 0.0 copy-start
  410.1 2.2 copy-done
  412.2 58.4 %shard_map.93 = f32[1024,1024]{1,0:T(8,128)S(1)} custom-call(f32[1024,1024]{1,0:T(8,128)S(1)} %copy-done), custom_call_target="tpu_custom_call" | custom-call | tf_op jit(solution)/shard_map/pallas_call | solution.py:94
  470.6 0.0 copy-start.1
  470.6 1.9 copy-done.1
  472.6 0.0 all-gather.3.cloned.1.call-update
  472.6 0.0 copy-start.2
  472.6 0.0 copy-start.5
  472.6 17.3 %fusion.16 = f32[1024,2048]{1,0:T(8,128)S(1)} fusion(f32[1024,1024]{1,0:T(8,128)} %copy-done.1, f32[1024,2048]{1,0:T(8,128)} %get-tuple-element.5), kind=kOutput, calls=%fused_computation.29 | convolution fusion | flops 12884901888 | bytes 20971520 | tf_op jit(solution)/shard_map/dot_general | solution.py:117
  489.9 0.0 copy-done.2
  489.9 0.0 copy-done.5
  490.0 6.8 %fusion.15 = f32[1024,1024]{0,1:T(8,128)S(1)} fusion(f32[1024,1024]{1,0:T(8,128)S(1)} %copy-done.5, f32[1024,1024]{1,0:T(8,128)S(1)} %copy-done.2), kind=kOutput, calls=%fused_computation.28 | convolution fusion | flops 6442450944 | bytes 12582912 | tf_op jit(solution)/shard_map/dot_general | solution.py:117
  496.8 1.9 copy-done.3
  498.7 17.3 %subtract_select_fusion = f32[1024,2048]{1,0:T(8,128)} fusion(f32[1024,2048]{1,0:T(8,128)} %param.6, pred[]{:T(512)S(6)} %eq.5, f32[1024,1024]{0,1:T(8,128)S(1)} %fusion.15, f32[1024,2048]{1,0:T(8,128)S(1)} %fusion.16), kind=kOutput, calls=%fused_computation.1 | convolution fusion | flops 12889096192 | bytes 29360128 | tf_op jit(solution)/shard_map/dot_general | solution.py:117
  516.0 5.4 copy.10
  521.4 4.9 slice_select_fusion
  526.4 4.0 pad_maximum_fusion
  530.3 2.9 multiply_subtract_fusion
  533.3 0.0 all-gather.3.cloned.1.call-done
  533.3 7.5 %fusion = f32[1024,768]{1,0:T(8,128)S(1)} fusion(f32[1024,1024]{1,0:T(8,128)} %copy-done.1, f32[1024,512]{1,0:T(8,128)S(1)} %multiply_subtract_fusion, f32[1024,256]{1,0:T(8,128)} %all-gather.3.cloned.1.call-done), kind=kOutput, calls=%fused_computation.5 | convolution fusion | flops 4832624640 | bytes 10485760 | tf_op jit(solution)/shard_map/dot_general | solution.py:117
  540.8 0.0 copy-start.4
  540.9 0.2 slice.43
  541.1 0.0 copy-start.8
  541.1 0.1 slice.42
  541.2 1.8 copy-done.4
  543.0 2.0 fusion.4
  545.0 1.7 fusion.5
  546.8 2.6 convolution_add_fusion
  (11 shorter events, 0.0 us)
Async XLA Ops:
  7.2 109.8 %all-reduce.4.cloned.1.call-start = ((), (), s32[]{:S(2)}) async-start(), calls=%async_computation | async-start | bytes 8388608 | tf_op jit(solution)/shard_map/psum | solution.py:106
  12.2 0.9 copy-start.7
  12.2 1.7 copy-start.6
  12.2 378.3 %all-reduce.6.cloned.1.call-start = ((), (), s32[]{:S(2)}) async-start(), calls=%async_computation.3 | async-start | bytes 26738688 | tf_op jit(solution)/shard_map/psum | solution.py:106
  119.8 270.9 %copy-start.9 = (s32[2,512]{1,0:T(2,128)S(1)}, s32[2,512]{1,0:T(2,128)}, u32[]{:S(2)}) copy-start(s32[2,512]{1,0:T(2,128)} %param.8) | copy-start | bytes 12292
  119.8 270.9 %copy-start.10 = (s32[2,256]{1,0:T(2,128)S(1)}, s32[2,256]{1,0:T(2,128)}, u32[]{:S(2)}) copy-start(s32[2,256]{1,0:T(2,128)} %param.7) | copy-start | bytes 6148
  119.8 410.6 %all-gather.5.cloned.1.call-start = ((), (), s32[]{:S(2)}) async-start(), calls=%async_computation.2 | async-start | bytes 2621440 | tf_op jit(solution)/shard_map/all_gather | solution.py:145
  390.6 142.8 %all-gather.3.cloned.1.call-start = ((), (), s32[]{:S(2)}) async-start(), calls=%async_computation.1 | async-start | bytes 1310720 | tf_op jit(solution)/shard_map/all_gather | solution.py:144
  410.0 2.2 copy-start
  470.6 1.9 copy-start.1
  472.6 17.4 %copy-start.2 = (f32[1024,1024]{1,0:T(8,128)S(1)}, f32[1024,1024]{1,0:T(8,128)}, u32[]{:S(2)}) copy-start(f32[1024,1024]{1,0:T(8,128)} %copy-done.1) | copy-start | bytes 12582916
  472.6 17.4 %copy-start.5 = (f32[1024,1024]{1,0:T(8,128)S(1)}, f32[1024,1024]{1,0:T(8,128)}, u32[]{:S(2)}) copy-start(f32[1024,1024]{1,0:T(8,128)} %all-reduce.4.cloned.1.call-done) | copy-start | bytes 12582916
  496.8 2.0 copy-start.3
  540.8 2.2 copy-start.4
  541.1 5.7 %copy-start.8 = (f32[512,256]{1,0:T(8,128)S(1)}, f32[512,256]{1,0:T(8,128)}, u32[]{:S(2)}) copy-start(f32[512,256]{1,0:T(8,128)} %param.11) | copy-start | bytes 1572868
Sparse Core Ops, SparseCore 0:
  12.3 104.5 all-reduce.3
  120.4 270.1 all-reduce.5
  392.5 36.0 all-gather.4
  472.7 29.1 all-gather.2

commit v2 on v1

v2 whole, which is shorter than its diff:
```python
import functools
import math

import jax
import jax.numpy as jnp
from jax import lax
from jax.experimental import pallas as pl
from jax.experimental.pallas import tpu as pltpu
from jax.sharding import PartitionSpec as P

RANGE = 16
BLOCK = 128
GROUP = 8
HALVES = 2
MESH = pl.DeviceIdType.MESH


root_three = math.sqrt(3.0)


def invert_block(block):
    size = block.shape[0]
    groups = size // GROUP
    wide = (GROUP, size)
    rows = lax.broadcasted_iota(jnp.int32, wide, 0)
    columns = lax.broadcasted_iota(jnp.int32, wide, 1)
    left = [block[g * GROUP : (g + 1) * GROUP, :] for g in range(groups)]
    right = [jnp.where(columns == rows + g * GROUP, 1.0, 0.0) for g in range(groups)]
    below = [rows > k for k in range(GROUP)]
    here = [rows == k for k in range(GROUP)]
    for g in range(groups):
        first = g * GROUP
        more = g + 1 < groups
        own = [jnp.broadcast_to(left[g][:, first + k : first + k + 1], wide) for k in range(GROUP)]
        if more:
            following = [
                jnp.broadcast_to(left[g + 1][:, first + k : first + k + 1], wide) for k in range(GROUP)
            ]
        for k in range(GROUP):
            root = lax.rsqrt(jnp.broadcast_to(own[k][k : k + 1, :], wide))
            factor = jnp.where(below[k], own[k] * root, 0.0)
            row_left = jnp.broadcast_to(left[g][k : k + 1, :], wide) * root
            row_right = jnp.broadcast_to(right[g][k : k + 1, :], wide) * root
            if more:
                factor_next = following[k] * root
            for m in range(k + 1, GROUP):
                row = jnp.broadcast_to(own[m][k : k + 1, :], wide) * root
                own[m] = own[m] - factor * row
                if more:
                    following[m] = following[m] - factor_next * row
            left[g] = jnp.where(here[k], row_left, left[g] - factor * row_left)
            right[g] = jnp.where(here[k], row_right, right[g] - factor * row_right)
            if more:
                left[g + 1] = left[g + 1] - factor_next * row_left
                right[g + 1] = right[g + 1] - factor_next * row_right
        if g + 2 < groups:
            turned = left[g].T[(g + 2) * GROUP :, :]
            rest = groups - g - 2
            tall = (rest * GROUP, size)
            rest_left = jnp.concatenate(left[g + 2 :], axis=0)
            rest_right = jnp.concatenate(right[g + 2 :], axis=0)
            for k in range(GROUP):
                factor = jnp.broadcast_to(turned[:, k : k + 1], tall)
                rest_left = rest_left - factor * left[g][k : k + 1, :]
                rest_right = rest_right - factor * right[g][k : k + 1, :]
            for i in range(rest):
                left[g + 2 + i] = rest_left[i * GROUP : (i + 1) * GROUP, :]
                right[g + 2 + i] = rest_right[i * GROUP : (i + 1) * GROUP, :]
    return jnp.concatenate(right, axis=0)


def invert_step(j, work, inverse_ref):
    size = work.shape[0]
    at = pl.ds(pl.multiple_of(j * BLOCK, BLOCK), BLOCK)
    columns = lax.broadcasted_iota(jnp.int32, (BLOCK, size), 1)
    inverse = invert_block(work[at, at])
    pivot = jnp.dot(inverse, work[at, :], precision=lax.Precision.HIGHEST)
    work[at, :] = pivot
    work[at, at] = inverse
    inverse_ref[at, :] = jnp.where(columns < (j + 1) * BLOCK, work[at, :], 0.0)


def update_step(j, work):
    size = work.shape[0]
    at = pl.ds(pl.multiple_of(j * BLOCK, BLOCK), BLOCK)

    @pl.loop(j + 1, size // BLOCK)
    def _(i):
        to = pl.ds(pl.multiple_of(i * BLOCK, BLOCK), BLOCK)
        factor = work[at, to]
        work[to, at] = jnp.zeros((BLOCK, BLOCK), jnp.float32)
        work[to, :] = work[to, :] - lax.dot_general(
            factor, work[at, :], (((0,), (0,)), ((), ())), precision=lax.Precision.HIGHEST
        )


def pick(index, table):
    found = 0
    for place, value in enumerate(table):
        found = found + jnp.where(index == place, value, 0)
    return found


def exchange_kernel(
    shape, cov, slab, panel, top, rhs, inverse, work, made, local_sem,
    panel_recv, left_recv, right_recv, inv_recv, slab_recv,
    panel_send, left_send, right_send, inv_send, slab_send,
):
    row_count, col_count = shape
    row, col = lax.axis_index("row"), lax.axis_index("col")
    size = panel.shape[0]
    count = size // BLOCK
    slab_rows = slab.shape[0]
    even = lax.rem(row, 2) == 0
    odd = jnp.logical_not(even)
    mate = row + 1 - 2 * lax.rem(row, 2)
    is_lead = jnp.logical_and(row == 0, col == 0)
    both = jnp.logical_and
    has_down = row + 2 < row_count

    barrier = pltpu.get_barrier_semaphore()

    def greet(r, c):
        pl.semaphore_signal(barrier, inc=1, device_id=(r, c), device_id_type=MESH)

    for shift in range(1, col_count):
        greet(row, lax.rem(col + shift, col_count))
    greet(mate, col)
    pl.when(row >= 2)(lambda: greet(row - 2, col))
    pl.when(has_down)(lambda: greet(row + 2, col))
    pl.semaphore_wait(barrier, col_count + jnp.where(row >= 2, 1, 0) + jnp.where(has_down, 1, 0))

    pending = []

    def send(condition, source, target, send_sem, recv_sem, r, c, waited=None):
        def make():
            return pltpu.make_async_remote_copy(
                src_ref=source, dst_ref=target, send_sem=send_sem, recv_sem=recv_sem,
                device_id=(r, c), device_id_type=MESH,
            )

        pl.when(condition)(lambda: make().start())
        if waited is None:
            pending.append((condition, make))
        elif waited is not False:
            pending.append((waited, make))

    def arrive(condition, target, recv_sem):
        def wait():
            pltpu.make_async_copy(target, target, recv_sem).wait()

        pl.when(condition)(wait)

    order = [i ^ (i >> 1) for i in range(col_count)]
    if sorted(order) != list(range(col_count)):
        order = list(range(col_count))
    onward, backward = [0] * col_count, [0] * col_count
    for i in range(col_count):
        onward[order[i]] = order[(i + 1) % col_count]
        backward[order[i]] = order[(i - 1) % col_count]
    next_col = jnp.where(even, pick(col, onward), pick(col, backward))

    def rows_of(t):
        return pl.ds(t * BLOCK, BLOCK)

    lead_cols, right_cols = pl.ds(0, size), pl.ds(size, top.shape[1] - size)

    def send_panel(condition, source, t):
        go = both(condition, next_col != 0)
        at = rows_of(t)
        send(go, source.at[at, lead_cols], panel.at[at], panel_send.at[t], panel_recv.at[t], row, next_col)

    def send_top(row_zero, t):
        at = rows_of(t)
        source = cov if row_zero else top
        here = row == 0 if row_zero else row > 0
        left, right = (at, lead_cols), (at, right_cols)
        go = both(here, even)
        send(both(go, has_down), source.at[left], top.at[left], left_send.at[0, t], left_recv.at[t], row + 2, col)
        send(go, source.at[left], top.at[left], left_send.at[1, t], left_recv.at[t], mate, col)
        if row_zero:
            send(here, source.at[right], top.at[right], right_send.at[0, t], right_recv.at[t], mate, col)
        else:
            go = both(here, odd)
            send(both(go, has_down), source.at[right], top.at[right], right_send.at[1, t], right_recv.at[t], row + 2, col)
            send(both(go, row > 1), source.at[right], top.at[right], right_send.at[2, t], right_recv.at[t], mate, col)

    levels = 0
    while (1 << levels) < col_count:
        levels += 1

    def send_inverse(condition, source, j, half, waits):
        at = (pl.ds(j * BLOCK + half * (BLOCK // HALVES), BLOCK // HALVES), pl.ds(0, (j + 1) * BLOCK))
        number = j * HALVES + half

        def to(where, slot, r, c):
            where = both(even, where)
            send(
                both(condition, where), source.at[at], inverse.at[at], inv_send.at[slot, number],
                inv_recv.at[number], r, c, where if waits else False,
            )

        to(both(col == 0, has_down), 0, row + 2, col)
        for level in range(levels):
            child = col + (1 << level)
            to(both(col < (1 << level), child < col_count), 1 + level, row, child)
        to(even, 1 + levels, mate, col)

    def slab_at(c):
        return rhs.at[pl.ds(pl.multiple_of(c * slab_rows, slab_rows), slab_rows)]

    lead_copy = pltpu.make_async_copy(cov.at[:, lead_cols], work, local_sem.at[0])
    panel_copy = pltpu.make_async_copy(cov.at[:, lead_cols], panel, local_sem.at[1])
    top_copy = pltpu.make_async_copy(cov, top, local_sem.at[2])
    slab_copy = pltpu.make_async_copy(slab, slab_at(col), local_sem.at[3])
    made_copy = pltpu.make_async_copy(made, inverse, local_sem.at[4])

    def send_slab(condition, source):
        own = slab_at(col)
        send(both(condition, has_down), source, own, slab_send.at[0], slab_recv.at[col], row + 2, col)
        for shift in range(1, col_count):
            send(condition, source, own, slab_send.at[shift], slab_recv.at[col], row, lax.rem(col + shift, col_count))
        send(condition, source, own, slab_send.at[col_count], slab_recv.at[col], mate, col)

    pl.when(is_lead)(lambda: lead_copy.start())
    for t in range(count):
        send_panel(col == 0, cov, t)
        send_top(True, t)
        if t == 0:
            send_slab(row == 0, slab)
    pl.when(col == 0)(lambda: panel_copy.start())
    pl.when(row == 0)(lambda: top_copy.start())
    pl.when(row == 0)(lambda: slab_copy.start())

    @pl.when(is_lead)
    def _():
        lead_copy.wait()

        @pl.loop(0, count)
        def _(j):
            invert_step(j, work, made)
            for step in range(count):

                @pl.when(j == step)
                def _():
                    for half in range(HALVES):
                        send_inverse(is_lead, made, step, half, False)

            update_step(j, work)

        made_copy.start()

    follows = jnp.logical_not(is_lead)
    lower = both(even, row > 0)
    for t in range(count):
        arrive(col > 0, panel.at[rows_of(t)], panel_recv.at[t])
        send_panel(col > 0, panel, t)
        for half in range(HALVES):
            at = (pl.ds(t * BLOCK + half * (BLOCK // HALVES), BLOCK // HALVES), pl.ds(0, (t + 1) * BLOCK))
            arrive(follows, inverse.at[at], inv_recv.at[t * HALVES + half])
            send_inverse(follows, inverse, t, half, True)
        arrive(lower, top.at[rows_of(t), lead_cols], left_recv.at[t])
        arrive(odd, top.at[rows_of(t), right_cols], right_recv.at[t])
        send_top(False, t)
        if t == min(1, count - 1):
            arrive(lower, slab_at(col), slab_recv.at[col])
            send_slab(lower, slab_at(col))
    for shift in range(1, col_count):
        other = lax.rem(col + shift, col_count)
        arrive(even, slab_at(other), slab_recv.at[other])
        send(
            even, slab_at(other), slab_at(other), slab_send.at[col_count + shift], slab_recv.at[other], mate, col
        )
    for t in range(count):
        arrive(odd, top.at[rows_of(t), lead_cols], left_recv.at[t])
        arrive(lower, top.at[rows_of(t), right_cols], right_recv.at[t])
    for c in range(col_count):
        arrive(odd, slab_at(c), slab_recv.at[c])
    for condition, make in pending:
        pl.when(condition)(lambda make=make: make().wait_send())
    pl.when(is_lead)(lambda: made_copy.wait())
    pl.when(col == 0)(lambda: panel_copy.wait())
    pl.when(row == 0)(lambda: top_copy.wait())
    pl.when(row == 0)(lambda: slab_copy.wait())


def exchange(shape, covariance, slab):
    size = covariance.shape[0]
    count = size // BLOCK
    slots = shape[1].bit_length() + 2
    f32 = jnp.float32
    dma = pltpu.SemaphoreType.DMA
    anywhere = pl.BlockSpec(memory_space=pl.ANY)
    return pl.pallas_call(
        functools.partial(exchange_kernel, shape),
        out_shape=(
            jax.ShapeDtypeStruct((size, size), f32),
            jax.ShapeDtypeStruct(covariance.shape, f32),
            jax.ShapeDtypeStruct((slab.shape[0] * shape[1], slab.shape[1]), f32),
            jax.ShapeDtypeStruct((size, size), f32),
        ),
        in_specs=[anywhere] * 2,
        out_specs=[anywhere] * 4,
        scratch_shapes=[
            pltpu.VMEM((size, size), f32),
            pltpu.VMEM((size, size), f32),
            dma((5,)),
            dma((count,)),
            dma((count,)),
            dma((count,)),
            dma((count * HALVES,)),
            dma((shape[1],)),
            dma((count,)),
            dma((2, count)),
            dma((3, count)),
            dma((slots, count * HALVES)),
            dma((2 * shape[1],)),
        ],
        compiler_params=pltpu.CompilerParams(
            collective_id=0, has_side_effects=True, vmem_limit_bytes=48 * 2**20
        ),
    )(covariance, slab)


def matern_tile(first, second):
    delta_x = first[0][:, None] - second[0][None, :]
    delta_y = first[1][:, None] - second[1][None, :]
    scaled = jnp.sqrt(delta_x * delta_x + delta_y * delta_y) * (root_three / RANGE)
    return (1.0 + scaled) * jnp.exp(-scaled)


def dot(first, second, first_axis, second_axis):
    return lax.dot_general(
        first, second, (((first_axis,), (second_axis,)), ((), ())), precision=lax.Precision.HIGH
    )


def body(shape, covariance, obs_cells, pred_cells, targets, cross_sum, prior_mean):
    tile_size = covariance.shape[0]
    slab = targets.shape[0]
    row_index = lax.axis_index("row")
    column_index = lax.axis_index("col")
    kernel = matern_tile(obs_cells.astype(jnp.float32), pred_cells.astype(jnp.float32))
    stacked = jnp.concatenate([targets, kernel - cross_sum], axis=1)
    panel_in, top_cov, lead_stacked, inverse = exchange(shape, covariance, stacked)
    inverse = jnp.tril(inverse)
    panel_rows = dot(panel_in, inverse, 1, 1)
    panel_columns = dot(inverse, top_cov, 1, 0)
    updated = covariance - dot(panel_rows, panel_columns, 1, 0)
    updated = jnp.where(row_index == 0, jnp.zeros_like(updated), updated)
    first_tile = jnp.where(column_index == 0, panel_rows, updated[:, :tile_size])
    factor_state = lax.dynamic_update_slice(updated, first_tile, (0, 0))
    both = dot(inverse, lead_stacked, 1, 0)
    width = targets.shape[1]
    solved = both[:, :width]
    lifted = both[:, width:]
    my_rows = lax.dynamic_slice_in_dim(panel_rows, column_index * slab, slab, 0)
    my_solved = lax.dynamic_slice_in_dim(solved, column_index * slab, slab, 0)
    my_lifted = lax.dynamic_slice_in_dim(lifted, column_index * slab, slab, 0)
    reduced_targets = targets - dot(my_rows, solved, 1, 0)
    reduced_targets = jnp.where(row_index == 0, my_solved, reduced_targets)
    cross_next = cross_sum + dot(my_rows, lifted, 1, 0)
    cross_next = jnp.where(row_index == 0, my_lifted, cross_next)
    predicted = prior_mean + dot(lifted, solved, 0, 0)
    return (factor_state, reduced_targets, cross_next, predicted)


def solution(mesh):
    shape = (mesh.shape["row"], mesh.shape["col"])
    in_specs = (
        P("row", "col"),
        P(None, ("row", "col")),
        P(),
        P(("row", "col"), None),
        P(("row", "col"), None),
        P(),
    )
    out_specs = (P("row", "col"), P(("row", "col"), None), P(("row", "col"), None), P())
    return jax.shard_map(
        functools.partial(body, shape), mesh=mesh, in_specs=in_specs, out_specs=out_specs, check_vma=False)
```

time: 564 us -> 454 us (0.80)
  the two profiles are of different devices: /device:TPU:29 before, /device:TPU:0 now
where the time goes in v2:
time: 454 us
  Pallas kernels  388 us (85%)
  matrix products  54.4 us (12%)
  other arithmetic  9.44 us (2%)
    pallas_call x1, Pallas kernels, exchange(): pl.pallas_call(functools.partial(exchange_kernel, shape), out_shape=(jax....  388 us
    dot_general x7, matrix products, dot(): lax.dot_general(first, second, (((first_axis,), (second_axis,)), ((), ())...  54.4 us

profile of v2, /device:TPU:0, one launch (start us, length us, event | category | flops | bytes accessed | tf_op | source)
XLA Modules:
  0.0 453.8 jit_solution(7382470300650220964)
XLA Ops:
  0.6 0.7 convert_element_type.6
  1.3 0.7 convert_element_type.7
  2.0 1.4 multiply_subtract_fusion
  3.5 1.0 pad_maximum_fusion.slab
  4.5 388.1 %shard_map.93 = (f32[1024,1024]{1,0:T(8,128)}, f32[1024,2048]{1,0:T(8,128)}, f32[1024,768]{1,0:T(8,128)S(1)}, f32[1024,1024]{1,0:T(8,128)}) custom-call(f32[1024,2048]{1,0:T(8,128)} %cov.1, f32[256,768]{1,0:T(8,128)S(1)} %pad_maximum_fusion.slab), custom_call_target="tpu_custom_call" | custom-call | tf_op jit(solution)/shard_map/pallas_call | solution.py:294
  392.5 0.0 copy-start.5
  392.6 10.7 %fusion.6 = f32[1024,1024]{1,0:T(8,128)S(1)} fusion(f32[1024,1024]{1,0:T(8,128)} %get-tuple-element.8, f32[1024,1024]{1,0:T(8,128)} %get-tuple-element.9), kind=kOutput, calls=%fused_computation.7 | convolution fusion | flops 6444548096 | bytes 12582912 | tf_op jit(solution)/shard_map/dot_general | solution.py:333
  403.2 0.0 copy-done.5
  403.2 0.0 copy-start.4
  403.2 0.0 slice-start.1
  403.3 5.1 %fusion.2 = f32[1024,768]{1,0:T(8,128)S(1)} fusion(f32[1024,768]{1,0:T(8,128)S(1)} %get-tuple-element.11, f32[1024,1024]{1,0:T(8,128)S(1)} %copy-done.5), kind=kOutput, calls=%fused_computation.5 | convolution fusion | flops 4833935360 | bytes 10485760 | tf_op jit(solution)/shard_map/dot_general | solution.py:333
  408.4 0.0 copy-done.4
  408.4 0.0 copy-start
  408.4 0.0 slice-start.2
  408.4 15.7 %fusion.4 = f32[1024,2048]{1,0:T(8,128)} fusion(f32[1024,2048]{1,0:T(8,128)S(1)} %copy-done.4, f32[1024,1024]{1,0:T(8,128)S(1)} %copy-done.5), kind=kOutput, calls=%fused_computation.6 | convolution fusion | flops 12886999040 | bytes 20971520 | tf_op jit(solution)/shard_map/dot_general | solution.py:333
  424.2 0.0 slice-done.1
  424.2 0.0 slice-done.2
  424.2 16.8 %subtract_select_fusion = f32[1024,2048]{1,0:T(8,128)} fusion(f32[1024,2048]{1,0:T(8,128)S(1)} %bitcast.12, pred[]{:T(512)S(6)} %eq.8, f32[1024,1024]{1,0:T(8,128)S(1)} %fusion.6, f32[1024,2048]{1,0:T(8,128)} %fusion.4), kind=kOutput, calls=%fused_computation | convolution fusion | flops 12889096192 | bytes 29360128 | tf_op jit(solution)/shard_map/dot_general | solution.py:333
  441.0 0.0 copy-start.3
  441.0 5.6 %fusion = f32[1024,2048]{1,0:T(8,128)} fusion(f32[1024,2048]{1,0:T(8,128)} %subtract_select_fusion, f32[1024,1024]{1,0:T(8,128)S(1)} %fusion.6, pred[]{:T(512)S(6)} %eq.9), kind=kLoop, calls=%fused_computation.2 | loop fusion | flops 1048576 | bytes 12582913 | tf_op jit(solution)/shard_map/dynamic_update_slice | solution.py:352
  446.6 0.0 copy-done.3
  446.6 2.7 convolution_add_fusion
  449.3 0.0 copy-start.1
  449.3 0.0 copy-done
  449.3 0.0 copy-start.2
  449.3 0.3 slice.34
  449.6 0.7 copy-done.1
  450.3 0.0 slice-start
  450.3 2.0 fusion.11
  452.4 0.0 copy-done.2
  452.4 0.0 slice-done
  452.4 1.4 fusion.12
  (3 shorter events, 0.0 us)
Async XLA Ops:
  392.5 10.7 %copy-start.5 = (f32[1024,1024]{1,0:T(8,128)S(1)}, f32[1024,1024]{1,0:T(8,128)}, u32[]{:S(2)}) copy-start(f32[1024,1024]{1,0:T(8,128)} %get-tuple-element.9) | copy-start | bytes 12582916
  403.2 5.1 %copy-start.4 = (f32[1024,2048]{1,0:T(8,128)S(1)}, f32[1024,2048]{1,0:T(8,128)}, u32[]{:S(2)}) copy-start(f32[1024,2048]{1,0:T(8,128)} %get-tuple-element.10) | copy-start | bytes 25165828
  403.2 20.9 %slice-start.1 = ((s8[8388608]{0:T(1024)(128)(4,1)}), s8[4194304]{0:T(1024)(128)(4,1)S(1)}, s32[]{:S(2)}) async-start(s8[8388608]{0:T(1024)(128)(4,1)} %bitcast.11), calls=%async_computation.1 | async-start | bytes 8388608
  408.4 40.9 %copy-start = (f32[1024,768]{1,0:T(8,128)}, f32[1024,768]{1,0:T(8,128)S(1)}, u32[]{:S(2)}) copy-start(f32[1024,768]{1,0:T(8,128)S(1)} %fusion.2) | copy-start | bytes 9437188
  408.4 15.8 %slice-start.2 = ((s8[8388608]{0:T(1024)(128)(4,1)}), s8[4194304]{0:T(1024)(128)(4,1)S(1)}, s32[]{:S(2)}) async-start(s8[8388608]{0:T(1024)(128)(4,1)} %bitcast.11), calls=%async_computation.2 | async-start | bytes 8388608
  441.0 5.6 %copy-start.3 = (f32[512,256]{1,0:T(8,128)S(1)}, f32[512,256]{1,0:T(8,128)}, u32[]{:S(2)}) copy-start(f32[512,256]{1,0:T(8,128)} %param.11) | copy-start | bytes 1572868
  449.3 1.0 copy-start.1
  449.3 3.1 copy-start.2
  450.3 2.0 slice-start

commit v3 on v2

--- a/solution.py
+++ b/solution.py
@@ -102,7 +102,7 @@
 
 
 def exchange_kernel(
-    shape, cov, slab, panel, top, rhs, inverse, work, made, local_sem,
+    shape, cov, slab, panel, top, rhs, inverse, work, local_sem,
     panel_recv, left_recv, right_recv, inv_recv, slab_recv,
     panel_send, left_send, right_send, inv_send, slab_send,
 ):
@@ -165,38 +165,37 @@
 
     lead_cols, right_cols = pl.ds(0, size), pl.ds(size, top.shape[1] - size)
 
-    def send_panel(condition, source, t):
+    def send_panel(condition, t):
         go = both(condition, next_col != 0)
         at = rows_of(t)
-        send(go, source.at[at, lead_cols], panel.at[at], panel_send.at[t], panel_recv.at[t], row, next_col)
+        send(go, panel.at[at], panel.at[at], panel_send.at[t], panel_recv.at[t], row, next_col)
 
     def send_top(row_zero, t):
         at = rows_of(t)
-        source = cov if row_zero else top
         here = row == 0 if row_zero else row > 0
         left, right = (at, lead_cols), (at, right_cols)
         go = both(here, even)
-        send(both(go, has_down), source.at[left], top.at[left], left_send.at[0, t], left_recv.at[t], row + 2, col)
-        send(go, source.at[left], top.at[left], left_send.at[1, t], left_recv.at[t], mate, col)
+        send(both(go, has_down), top.at[left], top.at[left], left_send.at[0, t], left_recv.at[t], row + 2, col)
+        send(go, top.at[left], top.at[left], left_send.at[1, t], left_recv.at[t], mate, col)
         if row_zero:
-            send(here, source.at[right], top.at[right], right_send.at[0, t], right_recv.at[t], mate, col)
+            send(here, top.at[right], top.at[right], right_send.at[0, t], right_recv.at[t], mate, col)
         else:
             go = both(here, odd)
-            send(both(go, has_down), source.at[right], top.at[right], right_send.at[1, t], right_recv.at[t], row + 2, col)
-            send(both(go, row > 1), source.at[right], top.at[right], right_send.at[2, t], right_recv.at[t], mate, col)
+            send(both(go, has_down), top.at[right], top.at[right], right_send.at[1, t], right_recv.at[t], row + 2, col)
+            send(both(go, row > 1), top.at[right], top.at[right], right_send.at[2, t], right_recv.at[t], mate, col)
 
     levels = 0
     while (1 << levels) < col_count:
         levels += 1
 
-    def send_inverse(condition, source, j, half, waits):
+    def send_inverse(condition, j, half, waits):
         at = (pl.ds(j * BLOCK + half * (BLOCK // HALVES), BLOCK // HALVES), pl.ds(0, (j + 1) * BLOCK))
         number = j * HALVES + half
 
         def to(where, slot, r, c):
             where = both(even, where)
             send(
-                both(condition, where), source.at[at], inverse.at[at], inv_send.at[slot, number],
+                both(condition, where), inverse.at[at], inverse.at[at], inv_send.at[slot, number],
                 inv_recv.at[number], r, c, where if waits else False,
             )
 
@@ -213,9 +212,9 @@
     panel_copy = pltpu.make_async_copy(cov.at[:, lead_cols], panel, local_sem.at[1])
     top_copy = pltpu.make_async_copy(cov, top, local_sem.at[2])
     slab_copy = pltpu.make_async_copy(slab, slab_at(col), local_sem.at[3])
-    made_copy = pltpu.make_async_copy(made, inverse, local_sem.at[4])
-
-    def send_slab(condition, source):
+
+    def send_slab(condition):
+        source = slab_at(col)
         own = slab_at(col)
         send(both(condition, has_down), source, own, slab_send.at[0], slab_recv.at[col], row + 2, col)
         for shift in range(1, col_count):
@@ -223,14 +222,17 @@
         send(condition, source, own, slab_send.at[col_count], slab_recv.at[col], mate, col)
 
     pl.when(is_lead)(lambda: lead_copy.start())
-    for t in range(count):
-        send_panel(col == 0, cov, t)
-        send_top(True, t)
-        if t == 0:
-            send_slab(row == 0, slab)
     pl.when(col == 0)(lambda: panel_copy.start())
     pl.when(row == 0)(lambda: top_copy.start())
     pl.when(row == 0)(lambda: slab_copy.start())
+    pl.when(col == 0)(lambda: panel_copy.wait())
+    pl.when(row == 0)(lambda: top_copy.wait())
+    pl.when(row == 0)(lambda: slab_copy.wait())
+    for t in range(count):
+        send_panel(col == 0, t)
+        send_top(True, t)
+        if t == 0:
+            send_slab(row == 0)
 
     @pl.when(is_lead)
     def _():
@@ -238,33 +240,31 @@
 
         @pl.loop(0, count)
         def _(j):
-            invert_step(j, work, made)
+            invert_step(j, work, inverse)
             for step in range(count):
 
                 @pl.when(j == step)
                 def _():
                     for half in range(HALVES):
-                        send_inverse(is_lead, made, step, half, False)
+                        send_inverse(is_lead, step, half, False)
 
             update_step(j, work)
-
-        made_copy.start()
 
     follows = jnp.logical_not(is_lead)
     lower = both(even, row > 0)
     for t in range(count):
         arrive(col > 0, panel.at[rows_of(t)], panel_recv.at[t])
-        send_panel(col > 0, panel, t)
+        send_panel(col > 0, t)
         for half in range(HALVES):
             at = (pl.ds(t * BLOCK + half * (BLOCK // HALVES), BLOCK // HALVES), pl.ds(0, (t + 1) * BLOCK))
             arrive(follows, inverse.at[at], inv_recv.at[t * HALVES + half])
-            send_inverse(follows, inverse, t, half, True)
+            send_inverse(follows, t, half, True)
         arrive(lower, top.at[rows_of(t), lead_cols], left_recv.at[t])
         arrive(odd, top.at[rows_of(t), right_cols], right_recv.at[t])
         send_top(False, t)
         if t == min(1, count - 1):
             arrive(lower, slab_at(col), slab_recv.at[col])
-            send_slab(lower, slab_at(col))
+            send_slab(lower)
     for shift in range(1, col_count):
         other = lax.rem(col + shift, col_count)
         arrive(even, slab_at(other), slab_recv.at[other])
@@ -278,10 +278,6 @@
         arrive(odd, slab_at(c), slab_recv.at[c])
     for condition, make in pending:
         pl.when(condition)(lambda make=make: make().wait_send())
-    pl.when(is_lead)(lambda: made_copy.wait())
-    pl.when(col == 0)(lambda: panel_copy.wait())
-    pl.when(row == 0)(lambda: top_copy.wait())
-    pl.when(row == 0)(lambda: slab_copy.wait())
 
 
 def exchange(shape, covariance, slab):
@@ -300,11 +296,10 @@
             jax.ShapeDtypeStruct((size, size), f32),
         ),
         in_specs=[anywhere] * 2,
-        out_specs=[anywhere] * 4,
+        out_specs=[pl.BlockSpec(memory_space=pltpu.VMEM)] * 4,
         scratch_shapes=[
             pltpu.VMEM((size, size), f32),
-            pltpu.VMEM((size, size), f32),
-            dma((5,)),
+            dma((4,)),
             dma((count,)),
             dma((count,)),
             dma((count,)),

time: 454 us -> 339 us (0.75)
  the two profiles are of different devices: /device:TPU:0 before, /device:TPU:29 now
where the time goes in v3:
time: 339 us
  Pallas kernels  273 us (81%)
  matrix products  54.4 us (16%)
  other arithmetic  9.44 us (3%)
    pallas_call x1, Pallas kernels, exchange(): pl.pallas_call(functools.partial(exchange_kernel, shape), out_shape=(jax....  273 us
    dot_general x7, matrix products, dot(): lax.dot_general(first, second, (((first_axis,), (second_axis,)), ((), ())...  54.4 us

profile of v3, /device:TPU:29, one launch (start us, length us, event | category | flops | bytes accessed | tf_op | source)
XLA Modules:
  0.0 338.7 jit_solution(6982447795101619429)
XLA Ops:
  0.6 0.7 convert_element_type.6
  1.3 0.7 convert_element_type.7
  2.0 1.4 multiply_subtract_fusion
  3.5 1.0 pad_maximum_fusion.slab
  4.5 273.0 %shard_map.93 = (f32[1024,1024]{1,0:T(8,128)}, f32[1024,2048]{1,0:T(8,128)}, f32[1024,768]{1,0:T(8,128)S(1)}, f32[1024,1024]{1,0:T(8,128)}) custom-call(f32[1024,2048]{1,0:T(8,128)} %cov.1, f32[256,768]{1,0:T(8,128)S(1)} %pad_maximum_fusion.slab), custom_call_target="tpu_custom_call" | custom-call | tf_op jit(solution)/shard_map/pallas_call | solution.py:290
  277.5 0.0 copy-start.5
  277.5 10.7 %fusion.6 = f32[1024,1024]{1,0:T(8,128)S(1)} fusion(f32[1024,1024]{1,0:T(8,128)} %get-tuple-element.8, f32[1024,1024]{1,0:T(8,128)} %get-tuple-element.9), kind=kOutput, calls=%fused_computation.7 | convolution fusion | flops 6444548096 | bytes 12582912 | tf_op jit(solution)/shard_map/dot_general | solution.py:328
  288.1 0.0 copy-done.5
  288.2 0.0 copy-start.4
  288.2 0.0 slice-start.1
  288.2 5.1 %fusion.2 = f32[1024,768]{1,0:T(8,128)S(1)} fusion(f32[1024,768]{1,0:T(8,128)S(1)} %get-tuple-element.11, f32[1024,1024]{1,0:T(8,128)S(1)} %copy-done.5), kind=kOutput, calls=%fused_computation.5 | convolution fusion | flops 4833935360 | bytes 10485760 | tf_op jit(solution)/shard_map/dot_general | solution.py:328
  293.3 0.0 copy-done.4
  293.3 0.0 copy-start
  293.3 0.0 slice-start.2
  293.3 15.7 %fusion.4 = f32[1024,2048]{1,0:T(8,128)} fusion(f32[1024,2048]{1,0:T(8,128)S(1)} %copy-done.4, f32[1024,1024]{1,0:T(8,128)S(1)} %copy-done.5), kind=kOutput, calls=%fused_computation.6 | convolution fusion | flops 12886999040 | bytes 20971520 | tf_op jit(solution)/shard_map/dot_general | solution.py:328
  309.1 0.0 slice-done.1
  309.1 0.0 slice-done.2
  309.1 16.8 %subtract_select_fusion = f32[1024,2048]{1,0:T(8,128)} fusion(f32[1024,2048]{1,0:T(8,128)S(1)} %bitcast.12, pred[]{:T(512)S(6)} %eq.8, f32[1024,1024]{1,0:T(8,128)S(1)} %fusion.6, f32[1024,2048]{1,0:T(8,128)} %fusion.4), kind=kOutput, calls=%fused_computation | convolution fusion | flops 12889096192 | bytes 29360128 | tf_op jit(solution)/shard_map/dot_general | solution.py:328
  325.9 0.0 copy-start.3
  325.9 5.6 %fusion = f32[1024,2048]{1,0:T(8,128)} fusion(f32[1024,2048]{1,0:T(8,128)} %subtract_select_fusion, f32[1024,1024]{1,0:T(8,128)S(1)} %fusion.6, pred[]{:T(512)S(6)} %eq.9), kind=kLoop, calls=%fused_computation.2 | loop fusion | flops 1048576 | bytes 12582913 | tf_op jit(solution)/shard_map/dynamic_update_slice | solution.py:347
  331.6 0.0 copy-done.3
  331.6 2.7 convolution_add_fusion
  334.2 0.0 copy-start.1
  334.2 0.0 copy-done
  334.2 0.0 copy-start.2
  334.2 0.3 slice.34
  334.5 0.7 copy-done.1
  335.3 0.0 slice-start
  335.3 2.0 fusion.11
  337.3 0.0 copy-done.2
  337.3 0.0 slice-done
  337.3 1.4 fusion.12
  (3 shorter events, 0.0 us)
Async XLA Ops:
  277.5 10.7 %copy-start.5 = (f32[1024,1024]{1,0:T(8,128)S(1)}, f32[1024,1024]{1,0:T(8,128)}, u32[]{:S(2)}) copy-start(f32[1024,1024]{1,0:T(8,128)} %get-tuple-element.9) | copy-start | bytes 12582916
  288.2 5.1 %copy-start.4 = (f32[1024,2048]{1,0:T(8,128)S(1)}, f32[1024,2048]{1,0:T(8,128)}, u32[]{:S(2)}) copy-start(f32[1024,2048]{1,0:T(8,128)} %get-tuple-element.10) | copy-start | bytes 25165828
  288.2 20.9 %slice-start.1 = ((s8[8388608]{0:T(1024)(128)(4,1)}), s8[4194304]{0:T(1024)(128)(4,1)S(1)}, s32[]{:S(2)}) async-start(s8[8388608]{0:T(1024)(128)(4,1)} %bitcast.11), calls=%async_computation.1 | async-start | bytes 8388608
  293.3 40.9 %copy-start = (f32[1024,768]{1,0:T(8,128)}, f32[1024,768]{1,0:T(8,128)S(1)}, u32[]{:S(2)}) copy-start(f32[1024,768]{1,0:T(8,128)S(1)} %fusion.2) | copy-start | bytes 9437188
  293.3 15.8 %slice-start.2 = ((s8[8388608]{0:T(1024)(128)(4,1)}), s8[4194304]{0:T(1024)(128)(4,1)S(1)}, s32[]{:S(2)}) async-start(s8[8388608]{0:T(1024)(128)(4,1)} %bitcast.11), calls=%async_computation.2 | async-start | bytes 8388608
  325.9 5.6 %copy-start.3 = (f32[512,256]{1,0:T(8,128)S(1)}, f32[512,256]{1,0:T(8,128)}, u32[]{:S(2)}) copy-start(f32[512,256]{1,0:T(8,128)} %param.11) | copy-start | bytes 1572868
  334.2 1.0 copy-start.1
  334.2 3.1 copy-start.2
  335.3 2.0 slice-start

commit v4 on v3

--- a/solution.py
+++ b/solution.py
@@ -145,6 +145,12 @@
         elif waited is not False:
             pending.append((waited, make))
 
+    def gated(gate, waits):
+        def start(condition, *rest):
+            send(both(gate, condition), *rest, waited=condition if waits else False)
+
+        return start
+
     def arrive(condition, target, recv_sem):
         def wait():
             pltpu.make_async_copy(target, target, recv_sem).wait()
@@ -165,12 +171,12 @@
 
     lead_cols, right_cols = pl.ds(0, size), pl.ds(size, top.shape[1] - size)
 
-    def send_panel(condition, t):
+    def send_panel(condition, t, send=send):
         go = both(condition, next_col != 0)
         at = rows_of(t)
         send(go, panel.at[at], panel.at[at], panel_send.at[t], panel_recv.at[t], row, next_col)
 
-    def send_top(row_zero, t):
+    def send_top(row_zero, t, send=send):
         at = rows_of(t)
         here = row == 0 if row_zero else row > 0
         left, right = (at, lead_cols), (at, right_cols)
@@ -228,11 +234,14 @@
     pl.when(col == 0)(lambda: panel_copy.wait())
     pl.when(row == 0)(lambda: top_copy.wait())
     pl.when(row == 0)(lambda: slab_copy.wait())
-    for t in range(count):
-        send_panel(col == 0, t)
-        send_top(True, t)
-        if t == 0:
-            send_slab(row == 0)
+    send_panel(col == 0, 0)
+    send_top(True, 0)
+    send_slab(row == 0)
+
+    def send_sources(gate, t, waits):
+        if t < count:
+            send_panel(col == 0, t, gated(gate, waits))
+            send_top(True, t, gated(gate, waits))
 
     @pl.when(is_lead)
     def _():
@@ -247,6 +256,7 @@
                 def _():
                     for half in range(HALVES):
                         send_inverse(is_lead, step, half, False)
+                    send_sources(is_lead, step + 1, False)
 
             update_step(j, work)
 
@@ -259,10 +269,11 @@
             at = (pl.ds(t * BLOCK + half * (BLOCK // HALVES), BLOCK // HALVES), pl.ds(0, (t + 1) * BLOCK))
             arrive(follows, inverse.at[at], inv_recv.at[t * HALVES + half])
             send_inverse(follows, t, half, True)
+        send_sources(follows, t + 1, True)
         arrive(lower, top.at[rows_of(t), lead_cols], left_recv.at[t])
         arrive(odd, top.at[rows_of(t), right_cols], right_recv.at[t])
         send_top(False, t)
-        if t == min(1, count - 1):
+        if t == min(3, count - 1):
             arrive(lower, slab_at(col), slab_recv.at[col])
             send_slab(lower)
     for shift in range(1, col_count):

time: 339 us -> 267 us (0.79)
  Pallas kernels: 273 us -> 201 us
    pallas_call x1, Pallas kernels: 273 us -> 201 us  [exchange(): pl.pallas_call(functools.partial(exchange_kernel, shape), out_shape=(jax....]
where the time goes in v4:
time: 267 us
  Pallas kernels  201 us (75%)
  matrix products  54.4 us (20%)
  other arithmetic  9.44 us (4%)
    pallas_call x1, Pallas kernels, exchange(): pl.pallas_call(functools.partial(exchange_kernel, shape), out_shape=(jax....  201 us
    dot_general x7, matrix products, dot(): lax.dot_general(first, second, (((first_axis,), (second_axis,)), ((), ())...  54.4 us
    dynamic_update_slice x1, other arithmetic, body(): factor_state = lax.dynamic_update_slice(updated, first_tile, (0, 0))  5.63 us

profile of v4, /device:TPU:29, one launch (start us, length us, event | category | flops | bytes accessed | tf_op | source)
XLA Modules:
  0.0 266.6 jit_solution(8085051061841148866)
XLA Ops:
  0.6 0.7 convert_element_type.6
  1.3 0.7 convert_element_type.7
  2.0 1.4 multiply_subtract_fusion
  3.5 1.0 pad_maximum_fusion.slab
  4.5 200.9 %shard_map.93 = (f32[1024,1024]{1,0:T(8,128)}, f32[1024,2048]{1,0:T(8,128)}, f32[1024,768]{1,0:T(8,128)S(1)}, f32[1024,1024]{1,0:T(8,128)}) custom-call(f32[1024,2048]{1,0:T(8,128)} %cov.1, f32[256,768]{1,0:T(8,128)S(1)} %pad_maximum_fusion.slab), custom_call_target="tpu_custom_call" | custom-call | tf_op jit(solution)/shard_map/pallas_call | solution.py:301
  205.4 0.0 copy-start.5
  205.4 10.7 %fusion.6 = f32[1024,1024]{1,0:T(8,128)S(1)} fusion(f32[1024,1024]{1,0:T(8,128)} %get-tuple-element.8, f32[1024,1024]{1,0:T(8,128)} %get-tuple-element.9), kind=kOutput, calls=%fused_computation.7 | convolution fusion | flops 6444548096 | bytes 12582912 | tf_op jit(solution)/shard_map/dot_general | solution.py:339
  216.0 0.0 copy-done.5
  216.1 0.0 copy-start.4
  216.1 0.0 slice-start.1
  216.1 5.1 %fusion.2 = f32[1024,768]{1,0:T(8,128)S(1)} fusion(f32[1024,768]{1,0:T(8,128)S(1)} %get-tuple-element.11, f32[1024,1024]{1,0:T(8,128)S(1)} %copy-done.5), kind=kOutput, calls=%fused_computation.5 | convolution fusion | flops 4833935360 | bytes 10485760 | tf_op jit(solution)/shard_map/dot_general | solution.py:339
  221.2 0.0 copy-done.4
  221.2 0.0 copy-start
  221.2 0.0 slice-start.2
  221.2 15.7 %fusion.4 = f32[1024,2048]{1,0:T(8,128)} fusion(f32[1024,2048]{1,0:T(8,128)S(1)} %copy-done.4, f32[1024,1024]{1,0:T(8,128)S(1)} %copy-done.5), kind=kOutput, calls=%fused_computation.6 | convolution fusion | flops 12886999040 | bytes 20971520 | tf_op jit(solution)/shard_map/dot_general | solution.py:339
  237.0 0.0 slice-done.1
  237.0 0.0 slice-done.2
  237.0 16.8 %subtract_select_fusion = f32[1024,2048]{1,0:T(8,128)} fusion(f32[1024,2048]{1,0:T(8,128)S(1)} %bitcast.12, pred[]{:T(512)S(6)} %eq.8, f32[1024,1024]{1,0:T(8,128)S(1)} %fusion.6, f32[1024,2048]{1,0:T(8,128)} %fusion.4), kind=kOutput, calls=%fused_computation | convolution fusion | flops 12889096192 | bytes 29360128 | tf_op jit(solution)/shard_map/dot_general | solution.py:339
  253.8 0.0 copy-start.3
  253.8 5.6 %fusion = f32[1024,2048]{1,0:T(8,128)} fusion(f32[1024,2048]{1,0:T(8,128)} %subtract_select_fusion, f32[1024,1024]{1,0:T(8,128)S(1)} %fusion.6, pred[]{:T(512)S(6)} %eq.9), kind=kLoop, calls=%fused_computation.2 | loop fusion | flops 1048576 | bytes 12582913 | tf_op jit(solution)/shard_map/dynamic_update_slice | solution.py:358
  259.5 0.0 copy-done.3
  259.5 2.7 convolution_add_fusion
  262.1 0.0 copy-start.1
  262.1 0.0 copy-done
  262.1 0.0 copy-start.2
  262.1 0.3 slice.34
  262.4 0.7 copy-done.1
  263.2 0.0 slice-start
  263.2 2.0 fusion.11
  265.2 0.0 copy-done.2
  265.2 0.0 slice-done
  265.2 1.4 fusion.12
  (3 shorter events, 0.0 us)
Async XLA Ops:
  205.4 10.7 %copy-start.5 = (f32[1024,1024]{1,0:T(8,128)S(1)}, f32[1024,1024]{1,0:T(8,128)}, u32[]{:S(2)}) copy-start(f32[1024,1024]{1,0:T(8,128)} %get-tuple-element.9) | copy-start | bytes 12582916
  216.1 5.1 %copy-start.4 = (f32[1024,2048]{1,0:T(8,128)S(1)}, f32[1024,2048]{1,0:T(8,128)}, u32[]{:S(2)}) copy-start(f32[1024,2048]{1,0:T(8,128)} %get-tuple-element.10) | copy-start | bytes 25165828
  216.1 20.9 %slice-start.1 = ((s8[8388608]{0:T(1024)(128)(4,1)}), s8[4194304]{0:T(1024)(128)(4,1)S(1)}, s32[]{:S(2)}) async-start(s8[8388608]{0:T(1024)(128)(4,1)} %bitcast.11), calls=%async_computation.1 | async-start | bytes 8388608
  221.2 40.9 %copy-start = (f32[1024,768]{1,0:T(8,128)}, f32[1024,768]{1,0:T(8,128)S(1)}, u32[]{:S(2)}) copy-start(f32[1024,768]{1,0:T(8,128)S(1)} %fusion.2) | copy-start | bytes 9437188
  221.2 15.8 %slice-start.2 = ((s8[8388608]{0:T(1024)(128)(4,1)}), s8[4194304]{0:T(1024)(128)(4,1)S(1)}, s32[]{:S(2)}) async-start(s8[8388608]{0:T(1024)(128)(4,1)} %bitcast.11), calls=%async_computation.2 | async-start | bytes 8388608
  253.8 5.6 %copy-start.3 = (f32[512,256]{1,0:T(8,128)S(1)}, f32[512,256]{1,0:T(8,128)}, u32[]{:S(2)}) copy-start(f32[512,256]{1,0:T(8,128)} %param.11) | copy-start | bytes 1572868
  262.1 1.0 copy-start.1
  262.1 3.1 %copy-start.2 = (f32[256,256]{1,0:T(8,128)S(1)}, f32[256,256]{1,0:T(8,128)}, u32[]{:S(2)}) copy-start(f32[256,256]{1,0:T(8,128)} %param.9) | copy-start | bytes 786436
  263.2 2.0 slice-start
